TPU v7x, 32 devices: a whole 2x2x4 slice. The times are simulated.
32 devices in a mesh: leaf: 8 (over z, y), panel: 4 (over x, core).
Axes of the slice: x: 2, y: 2, z: 4, core: 2. Of those that a mesh axis runs over, the one named last changes fastest.
Arguments:
- border: bfloat16 [8, 128, 8192], P('leaf', 'panel'), may hold values from -0.1875 to 0.1875
- solution: bfloat16 [8, 128, 128], P('leaf', 'panel'), may hold values from -6 to 6
- winv_top: bfloat16 [4096, 4096], P(None, ('leaf', 'panel')), as said below
- winv_mid: bfloat16 [4096, 8192], P(None, ('leaf', 'panel')), as said below
- coupling: bfloat16 [8192, 4096], P(('leaf', 'panel')), may hold values from -0.0625 to 0.0625
Outputs:
- top_adjoint: float32 [4096, 128], P(('leaf', 'panel'))
- mid_adjoint: float32 [8192, 128], P(('leaf', 'panel'))
Inputs may be any that keep to these rules, and one draw needn't show every extreme that they name: `winv_top`: each 4096 x 4096 block of the factor is lower triangular with a positive diagonal. `winv_mid`: each 4096 x 4096 block of the factor is lower triangular with a positive diagonal.
All inputs are finite; a program needn't handle non-finite values.
Results may differ from a plain program's by a relative error of at most 0.0003.
Values sent between devices are 32-bit elements; how exact they have to be, the bound alone decides.
No kernel may reach another device: no remote copies, remote signals or barrier semaphores. Data moves between devices by JAX's collectives and lax.ppermute only.
A program may use at most 64 MiB of HBM per device.

v0:
```python
import jax
import jax.numpy as jnp
from jax import lax
from jax.sharding import PartitionSpec as P


def from_partner(value, axis, stride):
    mask = 2**stride
    pairs = [(source, source ^ mask) for source in range(lax.axis_size(axis))]
    return lax.ppermute(value, axis, pairs)


def split_half(buffer, chosen):
    half_rows = buffer.shape[0] // 2
    kept_half = lax.dynamic_slice_in_dim(buffer, chosen * half_rows, half_rows, 0)
    sent_half = lax.dynamic_slice_in_dim(buffer, (1 - chosen) * half_rows, half_rows, 0)
    return (kept_half, sent_half)


def split_parity(buffer, chosen):
    paired = buffer.reshape(buffer.shape[0] // 2, 2, buffer.shape[1])
    even_rows = paired[:, 0]
    odd_rows = paired[:, 1]
    kept_rows = jnp.where(chosen == 0, even_rows, odd_rows)
    sent_rows = jnp.where(chosen == 0, odd_rows, even_rows)
    return (kept_rows, sent_rows)


def partner_halving(mid_part, leaf_id, leaf_bits):
    for bit_pos in reversed(range(leaf_bits)):
        chosen = leaf_id >> bit_pos & 1
        outgoing = []
        if bit_pos < leaf_bits - 1:
            mid_part, sent_mid = split_half(mid_part, chosen)
            outgoing.append(sent_mid)
        if outgoing:
            received = from_partner(outgoing[0], "leaf", bit_pos)
            mid_part = mid_part + received
    return (None, mid_part)


def body(border, solution, winv_top, winv_mid, coupling):
    leaves = lax.axis_size("leaf")
    leaf_bits = leaves.bit_length() - 1
    front_rows = winv_top.shape[0]
    leaf_id = lax.axis_index("leaf")
    contribution = lax.dot_general(
        border[0], solution[0], (((0,), (0,)), ((), ())), preferred_element_type=jnp.float32
    )
    top_part = contribution[:front_rows]
    mid_part = contribution[front_rows:]
    top_block = lax.psum_scatter(top_part, ("leaf", "panel"), scatter_dimension=0, tiled=True)
    nothing, mid_block = partner_halving(mid_part, leaf_id, leaf_bits)
    mid_block = lax.psum_scatter(mid_block, "panel", scatter_dimension=0, tiled=True)
    top_factor = winv_top.astype(jnp.float32)
    top_inner = lax.psum(
        jnp.dot(top_factor, top_block, precision=lax.Precision.HIGHEST), ("leaf", "panel")
    )
    top_adjoint = jnp.dot(top_factor.T, top_inner, precision=lax.Precision.HIGHEST)
    top_whole = lax.all_gather(top_adjoint, ("leaf", "panel"), axis=0, tiled=True)
    couple = coupling.astype(jnp.float32)
    mid_rhs = mid_block - jnp.dot(couple, top_whole, precision=lax.Precision.HIGHEST)
    mid_factor = winv_mid.astype(jnp.float32)
    group_block = jnp.dot(mid_factor, mid_rhs, precision=lax.Precision.HIGHEST)
    for bit_pos in reversed(range(leaf_bits - 1)):
        chosen = leaf_id >> bit_pos & 1
        kept_rows, sent_rows = split_parity(group_block, chosen)
        group_block = kept_rows + from_partner(sent_rows, "leaf", bit_pos)
    group_block = lax.psum(group_block, "panel")
    for bit_pos in range(leaf_bits - 1):
        chosen = leaf_id >> bit_pos & 1
        received = from_partner(group_block, "leaf", bit_pos)
        even_rows = jnp.where(chosen == 0, group_block, received)
        odd_rows = jnp.where(chosen == 0, received, group_block)
        group_block = jnp.stack([even_rows, odd_rows], 1).reshape(
            2 * group_block.shape[0], group_block.shape[1]
        )
    mid_adjoint = jnp.dot(mid_factor.T, group_block, precision=lax.Precision.HIGHEST)
    return (top_adjoint, mid_adjoint)


def solution(mesh):
    placed = (
        P("leaf", "panel", None),
        P("leaf", "panel", None),
        P(None, ("leaf", "panel")),
        P(None, ("leaf", "panel")),
        P(("leaf", "panel"), None),
    )
    return jax.shard_map(
        body,
        mesh=mesh,
        in_specs=placed,
        out_specs=(P(("leaf", "panel"), None), P(("leaf", "panel"), None)),
        check_vma=False,
    )
```

profile of v0, /device:TPU:0, one launch (start us, length us, event | category | flops | bytes accessed | tf_op | source)
XLA Modules:
  0.0 497.6 jit_solution(6646716508471507123)
XLA Ops:
  8.0 0.0 reduce-scatter.3.cloned.1.call-start
  8.1 1.9 fusion
  10.0 2.2 fusion.4
  12.3 0.0 all-reduce.3.cloned.1.call-start
  12.3 139.4 %reduce-scatter.3.cloned.1.call-done = f32[128,128]{1,0:T(8,128)} async-done(((f32[4096,128]{1,0:T(8,128)}), f32[128,128]{1,0:T(8,128)}) %reduce-scatter.3.cloned.1.call-update) | async-done | bytes 65552 | tf_op jit(solution)/shard_map/reduce_scatter | solution.py:52
  151.7 3.2 convolution_bitcast_fusion.1
  155.0 0.0 all-gather.2.cloned.1.call-start
  155.0 132.8 %all-reduce.3.cloned.1.call-done = f32[4096,128]{0,1:T(8,128)} async-done(((f32[4096,128]{0,1:T(8,128)}), f32[4096,128]{0,1:T(8,128)}) %all-reduce.3.cloned.1.call-update) | async-done | bytes 2097168 | tf_op jit(solution)/shard_map/psum | solution.py:56
  287.8 3.3 convolution_bitcast_fusion.4
  291.2 0.0 reduce-scatter.5.cloned.1.call-start
  291.2 1.3 constant_dynamic-slice_fusion.1
  292.5 1.4 collective-permute-start
  294.0 23.7 %collective-permute-done = f32[2048,128]{1,0:T(8,128)} collective-permute-done((f32[2048,128]{1,0:T(8,128)S(1)}, f32[2048,128]{1,0:T(8,128)}, u32[]{:S(2)}, u32[]{:S(2)}) %collective-permute-start) | collective-permute-done | bytes 1048608 | tf_op jit(solution)/shard_map/ppermute | solution.py:10
  317.7 1.6 dynamic-slice_add_fusion
  319.3 0.9 constant_dynamic-slice_fusion
  320.2 1.4 collective-permute-start.1
  321.6 10.6 %collective-permute-done.1 = f32[1024,128]{1,0:T(8,128)} collective-permute-done((f32[1024,128]{1,0:T(8,128)}, f32[1024,128]{1,0:T(8,128)}, u32[]{:S(2)}, u32[]{:S(2)}) %collective-permute-start.1) | collective-permute-done | bytes 524320 | tf_op jit(solution)/shard_map/ppermute | solution.py:10
  332.2 1.9 dynamic-slice_add_fusion.1
  334.1 0.0 reduce-scatter.5.cloned.1.call-update
  334.1 0.0 all-reduce.5.cloned.1.call-start
  334.2 13.9 %all-gather.2.cloned.1.call-done = f32[4096,128]{0,1:T(8,128)} async-done(((f32[128,128]{0,1:T(8,128)}), f32[4096,128]{0,1:T(8,128)}) %all-gather.2.cloned.1.call-update) | async-done | bytes 2097168 | tf_op jit(solution)/shard_map/all_gather | solution.py:60
  348.1 4.2 convolution_bitcast_fusion.3
  352.3 2.5 reduce-scatter.5.cloned.1.call-done
  354.8 4.5 convolution_bitcast_fusion
  359.3 2.9 copy.17
  362.2 4.7 broadcast_select_fusion
  366.9 1.5 collective-permute-start.2
  368.4 23.6 %collective-permute-done.2 = f32[2048,128]{1,0:T(8,128)} collective-permute-done((f32[2048,128]{1,0:T(8,128)}, f32[2048,128]{1,0:T(8,128)}, u32[]{:S(2)}, u32[]{:S(2)}) %collective-permute-start.2) | collective-permute-done | bytes 1048608 | tf_op jit(solution)/shard_map/ppermute | solution.py:10
  392.0 1.3 add.38
  393.4 0.8 broadcast_select_fusion.2
  394.1 1.6 collective-permute-start.3
  395.7 11.2 %collective-permute-done.3 = f32[1024,128]{1,0:T(8,128)S(1)} collective-permute-done((f32[1024,128]{1,0:T(8,128)S(1)}, f32[1024,128]{1,0:T(8,128)S(1)}, u32[]{:S(2)}, u32[]{:S(2)}) %collective-permute-start.3) | collective-permute-done | bytes 524320 | tf_op jit(solution)/shard_map/ppermute | solution.py:10
  406.9 0.9 add.39
  407.7 0.0 all-reduce.5.cloned.1.call-update
  407.8 33.4 %all-reduce.5.cloned.1.call-done = f32[1024,128]{1,0:T(8,128)} async-done(((f32[1024,128]{1,0:T(8,128)}), f32[1024,128]{1,0:T(8,128)}) %all-reduce.5.cloned.1.call-update) | async-done | bytes 524304 | tf_op jit(solution)/shard_map/psum | solution.py:69
  441.1 1.5 collective-permute-start.4
  442.6 11.0 %collective-permute-done.4 = f32[1024,128]{1,0:T(8,128)S(1)} collective-permute-done((f32[1024,128]{1,0:T(8,128)}, f32[1024,128]{1,0:T(8,128)S(1)}, u32[]{:S(2)}, u32[]{:S(2)}) %collective-permute-start.4) | collective-permute-done | bytes 524320 | tf_op jit(solution)/shard_map/ppermute | solution.py:10
  453.7 1.1 select_bitcast_fusion.3
  454.8 0.1 pad_maximum_fusion.1
  454.9 0.8 copy.18
  455.7 1.8 collective-permute-start.5
  457.5 0.7 copy.20
  458.2 20.5 %collective-permute-done.5 = f32[2048,128]{1,0:T(8,128)} collective-permute-done((f32[2048,128]{1,0:T(8,128)S(1)}, f32[2048,128]{1,0:T(8,128)}, u32[]{:S(2)}, u32[]{:S(2)}) %collective-permute-start.5) | collective-permute-done | bytes 1048608 | tf_op jit(solution)/shard_map/ppermute | solution.py:10
  478.8 1.4 select_bitcast_fusion.1
  480.1 0.1 pad_maximum_fusion
  480.3 7.6 %copy.19 = f32[2048,2,128]{2,1,0:T(2,128)S(1)} copy(f32[2048,2,128]{2,0,1:T(8,128)S(1)} %pad_maximum_fusion) | data formatting | bytes 4194304 | tf_op jit(solution)/shard_map/stack | solution.py:75
  487.9 1.9 convolution_bitcast_fusion.2
  489.8 0.8 copy.21
  (9 shorter events, 0.1 us)
Async XLA Ops:
  8.0 346.8 %copy-start = (bf16[4096,256]{1,0:T(8,128)(2,1)S(1)}, bf16[4096,256]{1,0:T(8,128)(2,1)}, u32[]{:S(2)}) copy-start(bf16[4096,256]{1,0:T(8,128)(2,1)} %param.8) | copy-start | bytes 6291460
  8.0 143.7 %reduce-scatter.3.cloned.1.call-start = ((), (), s32[]{:S(2)}) async-start(), calls=%async_computation.2 | async-start | bytes 2162688 | tf_op jit(solution)/shard_map/reduce_scatter | solution.py:52
  12.2 139.5 %copy-start.1 = (bf16[4096,128]{1,0:T(8,128)(2,1)S(1)}, bf16[4096,128]{1,0:T(8,128)(2,1)}, u32[]{:S(2)}) copy-start(bf16[4096,128]{1,0:T(8,128)(2,1)} %param.7) | copy-start | bytes 3145732
  12.3 275.5 %all-reduce.3.cloned.1.call-start = ((), (), s32[]{:S(2)}) async-start(), calls=%async_computation.3 | async-start | bytes 4194304 | tf_op jit(solution)/shard_map/psum | solution.py:56
  155.0 193.1 %all-gather.2.cloned.1.call-start = ((), (), s32[]{:S(2)}) async-start(), calls=%async_computation.5 | async-start | bytes 2162688 | tf_op jit(solution)/shard_map/all_gather | solution.py:60
  291.2 63.6 %reduce-scatter.5.cloned.1.call-start = ((), (), s32[]{:S(2)}) async-start(), calls=%async_computation.4 | async-start | bytes 655360 | tf_op jit(solution)/shard_map/reduce_scatter | solution.py:54
  292.5 25.2 %collective-permute-start = (f32[2048,128]{1,0:T(8,128)S(1)}, f32[2048,128]{1,0:T(8,128)}, u32[]{:S(2)}, u32[]{:S(2)}) collective-permute-start(f32[2048,128]{1,0:T(8,128)S(1)} %constant_dynamic-slice_fusion.1), channel_id=1, source_target_pairs={{0,8},{4,12},{8,0},{12,4},{16,24},{20,28},{24,16},{28,20},{1,9},{5... | collective-permute-start | bytes 3145736 | tf_op jit(solution)/shard_map/ppermute | solution.py:10
  320.2 12.0 %collective-permute-start.1 = (f32[1024,128]{1,0:T(8,128)}, f32[1024,128]{1,0:T(8,128)}, u32[]{:S(2)}, u32[]{:S(2)}) collective-permute-start(f32[1024,128]{1,0:T(8,128)} %constant_dynamic-slice_fusion), channel_id=1, source_target_pairs={{0,4},{4,0},{8,12},{12,8},{16,20},{20,16},{24,28},{28,24},{1,5},{5... | collective-permute-start | bytes 1572872 | tf_op jit(solution)/shard_map/ppermute | solution.py:10
  334.1 107.0 %all-reduce.5.cloned.1.call-start = ((), (), s32[]{:S(2)}) async-start(), calls=%async_computation.6 | async-start | bytes 1048576 | tf_op jit(solution)/shard_map/psum | solution.py:69
  366.9 25.1 %collective-permute-start.2 = (f32[2048,128]{1,0:T(8,128)}, f32[2048,128]{1,0:T(8,128)}, u32[]{:S(2)}, u32[]{:S(2)}) collective-permute-start(f32[2048,128]{1,0:T(8,128)} %bitcast.8), channel_id=1, source_target_pairs={{0,8},{4,12},{8,0},{12,4},{16,24},{20,28},{24,16},{28,20},{1,9},{5... | collective-permute-start | bytes 3145736 | tf_op jit(solution)/shard_map/ppermute | solution.py:10
  394.1 12.7 %collective-permute-start.3 = (f32[1024,128]{1,0:T(8,128)S(1)}, f32[1024,128]{1,0:T(8,128)S(1)}, u32[]{:S(2)}, u32[]{:S(2)}) collective-permute-start(f32[1024,128]{1,0:T(8,128)S(1)} %bitcast.48), channel_id=1, source_target_pairs={{0,4},{4,0},{8,12},{12,8},{16,20},{20,16},{24,28},{28,24},{1,5},{5... | collective-permute-start | bytes 1572872 | tf_op jit(solution)/shard_map/ppermute | solution.py:10
  441.1 12.5 %collective-permute-start.4 = (f32[1024,128]{1,0:T(8,128)}, f32[1024,128]{1,0:T(8,128)S(1)}, u32[]{:S(2)}, u32[]{:S(2)}) collective-permute-start(f32[1024,128]{1,0:T(8,128)} %all-reduce.5.cloned.1.call-done), channel_id=1, source_target_pairs={{0,4},{4,0},{8,12},{12,8},{16,20},{20,16},{24,28},{28,24},{1,5},{5... | collective-permute-start | bytes 1572872 | tf_op jit(solution)/shard_map/ppermute | solution.py:10
  454.8 2.7 copy-start.2
  455.7 23.1 %collective-permute-start.5 = (f32[2048,128]{1,0:T(8,128)S(1)}, f32[2048,128]{1,0:T(8,128)}, u32[]{:S(2)}, u32[]{:S(2)}) collective-permute-start(f32[2048,128]{1,0:T(8,128)S(1)} %bitcast.45), channel_id=1, source_target_pairs={{0,8},{4,12},{8,0},{12,4},{16,24},{20,28},{24,16},{28,20},{1,9},{5... | collective-permute-start | bytes 3145736 | tf_op jit(solution)/shard_map/ppermute | solution.py:10
Sparse Core Ops, SparseCore 0:
  12.4 139.3 reduce-scatter.2
  157.9 129.8 all-reduce.2
  291.7 56.3 all-gather.1
Sparse Core Ops, SparseCore 1:
  334.2 20.5 reduce-scatter.4
  407.8 33.2 all-reduce.4
where the time goes:
time: 498 us
  waiting for transfers between devices  423 us (85%)
  matrix products  19 us (4%)
  local copies, waits for them, and re-layouts  17.2 us (3%)
  between operations  15.3 us (3%)
  other arithmetic  13.9 us (3%)
  starting transfers between devices  9.32 us (2%)
    reduce_scatter x1, waiting for transfers between devices, body(): lax.psum_scatter(top_part, ('leaf', 'panel'), scatter_dimension=0, tiled=...  139 us
    psum x1, waiting for transfers between devices, body(): lax.psum(jnp.dot(top_factor, top_block, precision=lax.Precision.HIGHEST),...  133 us
    ppermute x6, waiting for transfers between devices, from_partner(): return lax.ppermute(value, axis, pairs)  101 us
    psum x1, waiting for transfers between devices, body(): group_block = lax.psum(group_block, 'panel')  33.4 us
    all_gather x1, waiting for transfers between devices, body(): lax.all_gather(top_adjoint, ('leaf', 'panel'), axis=0, tiled=True)  13.9 us
  transfers between devices with their start and end apart: 11, of which 11 were waited for; matrix products, arithmetic and copies ran while one was open for 2% of the time, Pallas kernels for 0%

commit v1 on v0

v1 whole, which is shorter than its diff:
```python
import functools

import jax
import jax.numpy as jnp
from jax import lax
from jax.experimental import pallas as pl
from jax.experimental.pallas import tpu as pltpu
from jax.sharding import PartitionSpec as P

AXES = ("leaf", "panel")
F32 = jnp.float32
BF16 = jnp.bfloat16
LANES = 128


def plain_body(border, solution, winv_top, winv_mid, coupling):
    leaves = lax.axis_size("leaf")
    panels = lax.axis_size("panel")
    half = leaves // 2
    leaf_id = lax.axis_index("leaf")
    front = winv_top.shape[0]
    top_cols = winv_top.shape[1]
    mid_cols = winv_mid.shape[1]
    contribution = lax.dot_general(
        border[0], solution[0], (((0,), (0,)), ((), ())), preferred_element_type=F32
    )
    groups = [list(range(half)), list(range(half, leaves))]
    device = leaf_id * panels + lax.axis_index("panel")
    in_half = device % (half * panels)
    top_load = lax.psum(contribution[:front], AXES)
    top_block = lax.dynamic_slice_in_dim(top_load, device * top_cols, top_cols, 0)
    mid_load = lax.psum(contribution[front:], "panel")
    mid_load = lax.psum(mid_load, "leaf", axis_index_groups=groups)
    mid_block = lax.dynamic_slice_in_dim(mid_load, in_half * mid_cols, mid_cols, 0)
    top_factor = winv_top.astype(F32)
    mid_factor = winv_mid.astype(F32)
    exact = lax.Precision.HIGHEST
    top_inner = lax.psum(jnp.dot(top_factor, top_block, precision=exact), AXES)
    top_adjoint = jnp.dot(top_factor.T, top_inner, precision=exact)
    top_whole = lax.all_gather(top_adjoint, AXES, axis=0, tiled=True)
    mid_rhs = mid_block - jnp.dot(coupling.astype(F32), top_whole, precision=exact)
    mid_inner = lax.psum(jnp.dot(mid_factor, mid_rhs, precision=exact), "panel")
    mid_inner = lax.psum(mid_inner, "leaf", axis_index_groups=groups)
    mid_adjoint = jnp.dot(mid_factor.T, mid_inner, precision=exact)
    return top_adjoint, mid_adjoint


def swap(value, mask):
    count = lax.axis_size("leaf") * lax.axis_size("panel")
    return lax.ppermute(value, AXES, [(i, i ^ mask) for i in range(count)])


CORE, XBIT, YBIT, ZBIT = 1, 2, 4, 8


def coords():
    leaf = lax.axis_index("leaf")
    panel = lax.axis_index("panel")
    return leaf // 2, leaf % 2, panel // 2, panel % 2


def kernel_call(kernel, outs, ins, scratch=(), flops=0, limit=24):
    vmem = pl.BlockSpec(memory_space=pltpu.VMEM)
    size = lambda s: s.size * s.dtype.itemsize
    return pl.pallas_call(
        kernel,
        out_shape=[jax.ShapeDtypeStruct(*o) for o in outs],
        in_specs=[vmem] * len(ins),
        out_specs=[vmem] * len(outs),
        scratch_shapes=list(scratch),
        compiler_params=pltpu.CompilerParams(vmem_limit_bytes=limit * 2**20),
        cost_estimate=pl.CostEstimate(
            flops=flops,
            transcendentals=0,
            bytes_accessed=sum(map(size, ins))
            + sum(size(jax.ShapeDtypeStruct(*o)) for o in outs),
        ),
    )(*ins)


def split2(value):
    high = value.astype(BF16)
    low = (value - high.astype(F32)).astype(BF16)
    return high, low


def xor(a, k):
    return lax.bitwise_xor(a, jnp.int32(k))


def flip(a, k):
    return a + k - 2 * a * k if k else a


def zrel(z, k, nz):
    low, high = z % 2, z // 2
    if nz == 2:
        return flip(low, k)
    return flip(high, k // 2) * 2 + flip(low, k % 2)


def block_row(z, y, x, nz, rows, zk, yk, xk, colour):
    block = zrel(z, zk, nz) * 4 + flip(y, yk) * 2 + flip(x, xk)
    return pl.multiple_of(block * (2 * rows) + colour * rows, rows)


def prep_border(border_ref, sol_ref, *out_refs):
    z, y, x, c = coords()
    tops, mids = out_refs[:8], out_refs[8:]
    front = border_ref.shape[1] // 2
    sol = sol_ref[...].astype(F32)
    for rel in range(8):
        peer = flip(y, rel // 4) * 4 + flip(x, rel // 2 % 2) * 2 + flip(c, rel % 2)
        for k in range(4):
            cols = pl.ds(pl.multiple_of(k * 1024 + peer * 128, 128), 128)
            tops[rel][:, k * 128 : (k + 1) * 128] = border_ref[:, cols].astype(F32)
        tops[rel][:, 512:640] = sol
        for k in range(2):
            cols = pl.ds(pl.multiple_of(front + k * 2048 + peer * 256, 256), 256)
            mids[rel][:, k * 256 : (k + 1) * 256] = border_ref[:, cols].astype(F32)


def top_load_kernel(*refs):
    ins, outs, (rows_ref, sol_ref, sum_ref) = refs[:8], refs[8:13], refs[13:]
    z, y, x, c = coords()
    for i in range(8):
        rows_ref[i * 32 : (i + 1) * 32, :] = ins[i][:, :512].astype(BF16)
        sol_ref[i * 32 : (i + 1) * 32, :] = ins[i][:, 512:640].astype(BF16)
    sum_ref[...] = lax.dot_general(
        sol_ref[...], rows_ref[...], (((0,), (0,)), ((), ())), preferred_element_type=F32
    )
    for k in range(4):
        cols = pl.ds(pl.multiple_of(zrel(z, k, 4) * 128, 128), 128)
        outs[k][...] = sum_ref[:, cols].T
    outs[4][...] = sol_ref[...]


def mid_load_kernel(*refs):
    ins, sol_ref, outs, (rows_ref, sum_ref) = refs[:8], refs[8], refs[9:11], refs[11:]
    z, y, x, c = coords()
    for i in range(8):
        rows_ref[i * 32 : (i + 1) * 32, :] = ins[i][...].astype(BF16)
    sum_ref[...] = lax.dot_general(
        sol_ref[...], rows_ref[...], (((0,), (0,)), ((), ())), preferred_element_type=F32
    )
    for k in range(2):
        cols = pl.ds(pl.multiple_of(zrel(z, k, 2) * 256, 256), 256)
        outs[k][...] = sum_ref[:, cols].T


def halve_rows(w_ref, keep_ref, send_ref):
    z, y, x, c = coords()
    rows = w_ref.shape[0] // 2
    keep_ref[...] = w_ref[pl.ds(pl.multiple_of(c * rows, rows), rows), :]
    send_ref[...] = w_ref[pl.ds(pl.multiple_of((1 - c) * rows, rows), rows), :].astype(F32)


def halve_cols(w_ref, keep_ref, send_ref):
    z, y, x, c = coords()
    for i in range(w_ref.shape[1] // 256):
        here = slice(i * 128, (i + 1) * 128)
        kept = pl.multiple_of(i * 256 + c * 128, 128)
        sent = pl.multiple_of(i * 256 + (1 - c) * 128, 128)
        keep_ref[:, here] = w_ref[:, pl.ds(kept, 128)]
        send_ref[:, here] = w_ref[:, pl.ds(sent, 128)].astype(F32)


def join_cols(keep_ref, recv_ref, w_ref, t_ref):
    n = keep_ref.shape[1]
    w_ref[:, :n] = keep_ref[...]
    w_ref[:, n:] = recv_ref[...].astype(BF16)
    t_ref[:n, :] = keep_ref[...].T
    t_ref[n:, :] = recv_ref[...].astype(BF16).T


def join_rows(keep_ref, recv_ref, w_ref):
    n = keep_ref.shape[0]
    w_ref[:n, :] = keep_ref[...]
    w_ref[n:, :] = recv_ref[...].astype(BF16)


PLACES = [(xk, yk) for xk in range(2) for yk in range(2)]


def scatter_blocks(sum_ref, outs, nz, rows):
    z, y, x, c = coords()
    for colour in range(2):
        for p, (xk, yk) in enumerate(PLACES):
            for zk in range(nz):
                start = block_row(z, y, x, nz, rows, zk, yk, xk, colour)
                outs[colour * 4 + p][zk * rows : (zk + 1) * rows, :] = sum_ref[
                    pl.ds(start, rows), :
                ]


def gather_blocks(pieces, rhs_ref, nz, rows):
    z, y, x, c = coords()
    for colour in range(2):
        for p, (xk, yk) in enumerate(PLACES):
            for zk in range(nz):
                start = block_row(z, y, x, nz, rows, zk, yk, xk, colour)
                high, low = split2(pieces[colour * 4 + p][zk * rows : (zk + 1) * rows, :])
                rhs_ref[pl.ds(start, rows), :LANES] = high
                rhs_ref[pl.ds(start, rows), LANES:] = low


def forward(nz, rows, w_ref, *refs):
    vec, outs, (rhs_ref, sum_ref) = refs[:-10], refs[-10:-2], refs[-2:]
    if len(vec) == 2:
        pair = [vec[0][...], vec[1][...]]
    else:
        mine, theirs, part0, part1, recv0, recv1 = vec
        pair = [
            mine[...] - part0[...] - recv1[...],
            theirs[...] - part1[...] - recv0[...],
        ]
    n = pair[0].shape[0]
    for i in range(2):
        high, low = split2(pair[i])
        rhs_ref[i * n : (i + 1) * n, :LANES] = high
        rhs_ref[i * n : (i + 1) * n, LANES:] = low
    both = jnp.dot(w_ref[...], rhs_ref[...], preferred_element_type=F32)
    sum_ref[...] = both[:, :LANES] + both[:, LANES:]
    scatter_blocks(sum_ref, outs, nz, rows)


def backward(nz, rows, w_ref, *refs):
    pieces, (own_ref, other_ref), rhs_ref = refs[:8], refs[8:10], refs[10]
    gather_blocks(pieces, rhs_ref, nz, rows)
    both = jnp.dot(w_ref[...], rhs_ref[...], preferred_element_type=F32)
    total = both[:, :LANES] + both[:, LANES:]
    n = own_ref.shape[0]
    own_ref[...] = total[:n]
    other_ref[...] = total[n:]


def run_forward(w, vec, nz, rows):
    m, k = w.shape
    return kernel_call(
        functools.partial(forward, nz, rows),
        [((m // 8, LANES), F32)] * 8,
        [w, *vec],
        [pltpu.VMEM((k, 2 * LANES), BF16), pltpu.VMEM((m, LANES), F32)],
        flops=4 * m * k * LANES,
    )


def run_backward(w, pieces, nz, rows):
    m, k = w.shape
    return kernel_call(
        functools.partial(backward, nz, rows),
        [((m // 2, LANES), F32)] * 2,
        [w, *pieces],
        [pltpu.VMEM((k, 2 * LANES), BF16)],
        flops=4 * m * k * LANES,
    )


def plane_sum(pieces):
    a00, a01, a10, a11, b00, b01, b10, b11 = pieces
    ra = swap(a11, XBIT)
    rb = swap(b11, YBIT)
    qa = swap(a10, XBIT)
    qb = swap(b01, YBIT)
    sa = swap(a01 + ra, YBIT)
    sb = swap(b10 + rb, XBIT)
    return a00 + qa + sa, b00 + qb + sb


def plane_spread(a, b):
    ya = swap(a, YBIT)
    xb = swap(b, XBIT)
    xa = swap(a, XBIT)
    yb = swap(b, YBIT)
    return [a, ya, xa, swap(ya, XBIT), b, yb, xb, swap(xb, YBIT)]


def depth_sum(a, b, nz, rows):
    cut = lambda k: jnp.concatenate(
        [a[k * rows : (k + 1) * rows], b[k * rows : (k + 1) * rows]], 0
    )
    got = [swap(cut(k), ZBIT * k) for k in range(1, nz)]
    total = cut(0)
    for g in got:
        total = total + g
    return total


def depth_spread(own, nz, rows):
    parts = [own] + [swap(own, ZBIT * k) for k in range(1, nz)]
    a = jnp.concatenate([p[:rows] for p in parts], 0)
    b = jnp.concatenate([p[rows:] for p in parts], 0)
    return a, b


def everywhere(own, nz, rows):
    return plane_spread(*depth_spread(own, nz, rows))


def fast_body(border, solution, winv_top, winv_mid, coupling):
    front = winv_top.shape[0]
    half = front // 2
    out = kernel_call(
        prep_border,
        [((32, 640), F32)] * 8 + [((32, 512), F32)] * 8,
        [border[0], solution[0]],
    )
    tops, mids = out[:8], out[8:]
    tops = [tops[0]] + [swap(tops[r], r) for r in range(1, 8)]
    *loads, sol_all = kernel_call(
        top_load_kernel,
        [((128, LANES), F32)] * 4 + [((256, LANES), BF16)],
        tops,
        [
            pltpu.VMEM((256, 512), BF16),
            pltpu.VMEM((256, LANES), BF16),
            pltpu.VMEM((LANES, 512), F32),
        ],
        flops=2 * 256 * 512 * 128,
    )
    load = loads[0]
    for k in range(1, 4):
        load = load + swap(loads[k], ZBIT * k)
    load_other = swap(load, CORE)

    top_keep, top_send = kernel_call(
        halve_rows, [((half, 128), BF16), ((half, 128), F32)], [winv_top]
    )
    cou_keep, cou_send = kernel_call(
        halve_cols, [((256, half), BF16), ((256, half), F32)], [coupling]
    )
    mid_keep, mid_send = kernel_call(
        halve_rows, [((half, 256), BF16), ((half, 256), F32)], [winv_mid]
    )
    top_w, top_t = kernel_call(
        join_cols,
        [((half, 256), BF16), ((256, half), BF16)],
        [top_keep, swap(top_send, CORE)],
    )
    (cou_w,) = kernel_call(
        join_rows, [((512, half), BF16)], [cou_keep, swap(cou_send, CORE)]
    )
    mid_w, mid_t = kernel_call(
        join_cols,
        [((half, 512), BF16), ((512, half), BF16)],
        [mid_keep, swap(mid_send, CORE)],
    )

    pieces = run_forward(top_w, [load, load_other], 4, 64)
    inner = depth_sum(*plane_sum(pieces), 4, 64)
    own, other = run_backward(top_t, everywhere(inner, 4, 64), 4, 64)
    top_adjoint = own + swap(other, CORE)

    mids = [mids[0]] + [swap(mids[r], r) for r in range(1, 8)]
    mid0, mid1 = kernel_call(
        mid_load_kernel,
        [((256, LANES), F32)] * 2,
        [*mids, sol_all],
        [pltpu.VMEM((256, 512), BF16), pltpu.VMEM((LANES, 512), F32)],
        flops=2 * 256 * 512 * 128,
    )
    mid_load = mid0 + swap(mid1, ZBIT)
    mid_other = swap(mid_load, CORE)

    part0, part1 = run_backward(cou_w, everywhere(top_adjoint, 4, 64), 4, 64)
    vec = [mid_load, mid_other, part0, part1, swap(part0, CORE), swap(part1, CORE)]
    pieces = run_forward(mid_w, vec, 2, 128)
    inner = depth_sum(*plane_sum(pieces), 2, 128)
    own, other = run_backward(mid_t, everywhere(inner, 2, 128), 2, 128)
    return top_adjoint, own + swap(other, CORE)


def solution(mesh):
    placed = (
        P("leaf", "panel", None),
        P("leaf", "panel", None),
        P(None, AXES),
        P(None, AXES),
        P(AXES, None),
    )
    fits = mesh.shape["leaf"] == 8 and mesh.shape["panel"] == 4
    return jax.shard_map(
        fast_body if fits else plain_body,
        mesh=mesh,
        in_specs=placed,
        out_specs=(P(AXES, None), P(AXES, None)),
        check_vma=False,
    )
```

time: 498 us -> 159 us (0.32)
  waiting for transfers between devices: 423 us -> 76 us
  starting transfers between devices: 9.32 us -> 71 us
  matrix products: 19 us -> 0 us
  between operations: 15.3 us -> 1.12 us
  local copies, waits for them, and re-layouts: 17.2 us -> 3.08 us
  other arithmetic: 13.9 us -> 0.98 us
  Pallas kernels: 0 us -> 6.92 us
    psum x2 -> x0, waiting for transfers between devices: 166 us -> none  [the longest x1 133 us: body(): lax.psum(jnp.dot(top_factor, top_block, precision=lax.Precision.HIGHEST),...]
    reduce_scatter x2 -> x0, waiting for transfers between devices: 142 us -> none  [the longest x1 139 us: body(): lax.psum_scatter(top_part, ('leaf', 'panel'), scatter_dimension=0, tiled=...]
    ppermute x6 -> x68, starting transfers between devices: 9.11 us -> 71 us  [swap(): return lax.ppermute(value, AXES, [(i, i ^ mask) for i in range(count)])]
    ppermute x6 -> x68, waiting for transfers between devices: 101 us -> 76 us  [swap(): return lax.ppermute(value, AXES, [(i, i ^ mask) for i in range(count)])]
    dot_general x6 -> x0, matrix products: 19 us -> none  [the longest x1 4.51 us: body(): group_block = jnp.dot(mid_factor, mid_rhs, precision=lax.Precision.HIGHEST)]
    all_gather x1 -> x0, waiting for transfers between devices: 13.9 us -> none  [body(): lax.all_gather(top_adjoint, ('leaf', 'panel'), axis=0, tiled=True)]
    another operation x2 -> x0, local copies, waits for them, and re-layouts: 8.41 us -> none  [body(): jnp.stack([even_rows, odd_rows], 1)]
    pallas_call x0 -> x14, Pallas kernels: none -> 6.92 us  [kernel_call(): pl.pallas_call(kernel, out_shape=[jax.ShapeDtypeStruct(*o) for o in outs]...]
  transfers between devices with their start and end apart: 11 -> 68, of which waited for: 11 -> 42; matrix products, arithmetic and copies ran while one was open for 2% -> 0% of each run, Pallas kernels for 0% -> 3%
where the time goes in v1:
time: 159 us
  waiting for transfers between devices  76 us (48%)
  starting transfers between devices  71 us (45%)
  Pallas kernels  6.92 us (4%)
  local copies, waits for them, and re-layouts  3.08 us (2%)
    ppermute x68, waiting for transfers between devices, swap(): return lax.ppermute(value, AXES, [(i, i ^ mask) for i in range(count)])  76 us
    ppermute x68, starting transfers between devices, swap(): return lax.ppermute(value, AXES, [(i, i ^ mask) for i in range(count)])  71 us
    pallas_call x14, Pallas kernels, kernel_call(): pl.pallas_call(kernel, out_shape=[jax.ShapeDtypeStruct(*o) for o in outs]...  6.92 us
  transfers between devices with their start and end apart: 68, of which 42 were waited for; matrix products, arithmetic and copies ran while one was open for 0% of the time, Pallas kernels for 3%

profile of v1, /device:TPU:0, one launch (start us, length us, event | category | flops | bytes accessed | tf_op | source)
XLA Modules:
  0.0 159.1 jit_solution(17259498282936742830)
XLA Ops:
  4.5 2.9 %collective-permute-start.2 = (f32[32,640]{1,0:T(8,128)S(1)}, f32[32,640]{1,0:T(8,128)S(1)}, u32[]{:S(2)}, u32[]{:S(2)}) collective-permute-start(f32[32,640]{1,0:T(8,128)S(1)} %get-tuple-element.63), channel_id=1, source_target_pairs={{0,2},{1,3},{2,0},{3,1},{4,6},{5,7},{6,4},{7,5},{8,10},{9,11},{10,... | collective-permute-start | bytes 245768 | tf_op jit(solution)/shard_map/ppermute | solution.py:50
  7.4 1.5 collective-permute-start.4
  10.2 3.4 %collective-permute-start.6 = (f32[32,640]{1,0:T(8,128)S(1)}, f32[32,640]{1,0:T(8,128)S(1)}, u32[]{:S(2)}, u32[]{:S(2)}) collective-permute-start(f32[32,640]{1,0:T(8,128)S(1)} %get-tuple-element.67), channel_id=1, source_target_pairs={{0,6},{1,7},{2,4},{3,5},{4,2},{5,3},{6,0},{7,1},{8,14},{9,15},{10,... | collective-permute-start | bytes 245768 | tf_op jit(solution)/shard_map/ppermute | solution.py:50
  14.5 1.6 collective-permute-done.6.refs_6_
  16.1 2.4 %collective-permute-done.7.refs_7_ = f32[32,640]{1,0:T(8,128)S(1)} collective-permute-done((f32[32,640]{1,0:T(8,128)S(1)}, f32[32,640]{1,0:T(8,128)S(1)}, u32[]{:S(2)}, u32[]{:S(2)}) %collective-permute-start.7) | collective-permute-done | bytes 81952 | tf_op jit(solution)/shard_map/ppermute | solution.py:50
  18.8 3.7 %collective-permute-start.10 = (f32[128,128]{1,0:T(8,128)S(1)}, f32[128,128]{1,0:T(8,128)S(1)}, u32[]{:S(2)}, u32[]{:S(2)}) collective-permute-start(f32[128,128]{1,0:T(8,128)S(1)} %get-tuple-element.72), channel_id=1, source_target_pairs={{0,24},{1,25},{2,26},{3,27},{4,28},{5,29},{6,30},{7,31},{8,16},{9,... | collective-permute-start | bytes 196616 | tf_op jit(solution)/shard_map/ppermute | solution.py:50
  23.2 1.7 %collective-permute-done.10 = f32[128,128]{1,0:T(8,128)S(1)} collective-permute-done((f32[128,128]{1,0:T(8,128)S(1)}, f32[128,128]{1,0:T(8,128)S(1)}, u32[]{:S(2)}, u32[]{:S(2)}) %collective-permute-start.10) | collective-permute-done | bytes 65568 | tf_op jit(solution)/shard_map/ppermute | solution.py:50
  25.0 1.7 %collective-permute-done.8 = f32[128,128]{1,0:T(8,128)S(1)} collective-permute-done((f32[128,128]{1,0:T(8,128)S(1)}, f32[128,128]{1,0:T(8,128)S(1)}, u32[]{:S(2)}, u32[]{:S(2)}) %collective-permute-start.8) | collective-permute-done | bytes 65568 | tf_op jit(solution)/shard_map/ppermute | solution.py:50
  29.5 2.2 %collective-permute-start.13 = (f32[256,128]{1,0:T(8,128)S(1)}, f32[256,128]{1,0:T(8,128)S(1)}, u32[]{:S(2)}, u32[]{:S(2)}) collective-permute-start(f32[256,128]{1,0:T(8,128)S(1)} %get-tuple-element.76), channel_id=1, source_target_pairs={{0,2},{1,3},{2,0},{3,1},{4,6},{5,7},{6,4},{7,5},{8,10},{9,11},{10,... | collective-permute-start | bytes 393224 | tf_op jit(solution)/shard_map/ppermute | solution.py:50
  33.2 2.7 %collective-permute-done.13 = f32[256,128]{1,0:T(8,128)S(1)} collective-permute-done((f32[256,128]{1,0:T(8,128)S(1)}, f32[256,128]{1,0:T(8,128)S(1)}, u32[]{:S(2)}, u32[]{:S(2)}) %collective-permute-start.13) | collective-permute-done | bytes 131104 | tf_op jit(solution)/shard_map/ppermute | solution.py:50
  36.0 1.6 %collective-permute-start.14 = (f32[256,128]{1,0:T(8,128)S(1)}, f32[256,128]{1,0:T(8,128)S(1)}, u32[]{:S(2)}, u32[]{:S(2)}) collective-permute-start(f32[256,128]{1,0:T(8,128)S(1)} %add.70), channel_id=1, source_target_pairs={{0,4},{1,5},{2,6},{3,7},{4,0},{5,1},{6,2},{7,3},{8,12},{9,13},{10,... | collective-permute-start | bytes 393224 | tf_op jit(solution)/shard_map/ppermute | solution.py:50
  38.1 2.1 %collective-permute-start.17 = (f32[256,128]{1,0:T(8,128)S(1)}, f32[256,128]{1,0:T(8,128)S(1)}, u32[]{:S(2)}, u32[]{:S(2)}) collective-permute-start(f32[256,128]{1,0:T(8,128)S(1)} %add.73), channel_id=1, source_target_pairs={{0,2},{1,3},{2,0},{3,1},{4,6},{5,7},{6,4},{7,5},{8,10},{9,11},{10,... | collective-permute-start | bytes 393224 | tf_op jit(solution)/shard_map/ppermute | solution.py:50
  40.2 1.8 %collective-permute-done.14 = f32[256,128]{1,0:T(8,128)S(1)} collective-permute-done((f32[256,128]{1,0:T(8,128)S(1)}, f32[256,128]{1,0:T(8,128)S(1)}, u32[]{:S(2)}, u32[]{:S(2)}) %collective-permute-start.14) | collective-permute-done | bytes 131104 | tf_op jit(solution)/shard_map/ppermute | solution.py:50
  43.5 1.8 %collective-permute-start.18 = (f32[128,128]{1,0:T(8,128)S(1)}, f32[128,128]{1,0:T(8,128)S(1)}, u32[]{:S(2)}, u32[]{:S(2)}) collective-permute-start(f32[128,128]{1,0:T(8,128)S(1)} %pad_maximum_fusion.7), channel_id=1, source_target_pairs={{0,8},{1,9},{2,10},{3,11},{4,12},{5,13},{6,14},{7,15},{8,0},{9,1},... | collective-permute-start | bytes 196616 | tf_op jit(solution)/shard_map/ppermute | solution.py:50
  49.4 1.8 %collective-permute-start.33 = (f32[32,512]{1,0:T(8,128)S(1)}, f32[32,512]{1,0:T(8,128)S(1)}, u32[]{:S(2)}, u32[]{:S(2)}) collective-permute-start(f32[32,512]{1,0:T(8,128)S(1)} %get-tuple-element.89), channel_id=1, source_target_pairs={{0,2},{1,3},{2,0},{3,1},{4,6},{5,7},{6,4},{7,5},{8,10},{9,11},{10,... | collective-permute-start | bytes 196616 | tf_op jit(solution)/shard_map/ppermute | solution.py:50
  52.6 4.2 %collective-permute-done.21 = f32[128,128]{1,0:T(8,128)S(1)} collective-permute-done((f32[128,128]{1,0:T(8,128)S(1)}, f32[128,128]{1,0:T(8,128)S(1)}, u32[]{:S(2)}, u32[]{:S(2)}) %collective-permute-start.21) | collective-permute-done | bytes 65568 | tf_op jit(solution)/shard_map/ppermute | solution.py:50
  56.9 5.5 %collective-permute-done.22 = f32[128,128]{1,0:T(8,128)S(1)} collective-permute-done((f32[128,128]{1,0:T(8,128)S(1)}, f32[128,128]{1,0:T(8,128)S(1)}, u32[]{:S(2)}, u32[]{:S(2)}) %collective-permute-start.22) | collective-permute-done | bytes 65568 | tf_op jit(solution)/shard_map/ppermute | solution.py:50
  63.7 4.8 %collective-permute-done.23 = f32[128,128]{1,0:T(8,128)S(1)} collective-permute-done((f32[128,128]{1,0:T(8,128)S(1)}, f32[128,128]{1,0:T(8,128)S(1)}, u32[]{:S(2)}, u32[]{:S(2)}) %collective-permute-start.23) | collective-permute-done | bytes 65568 | tf_op jit(solution)/shard_map/ppermute | solution.py:50
  68.6 1.9 %collective-permute-start.35 = (f32[32,512]{1,0:T(8,128)S(1)}, f32[32,512]{1,0:T(8,128)S(1)}, u32[]{:S(2)}, u32[]{:S(2)}) collective-permute-start(f32[32,512]{1,0:T(8,128)S(1)} %get-tuple-element.91), channel_id=1, source_target_pairs={{0,4},{1,5},{2,6},{3,7},{4,0},{5,1},{6,2},{7,3},{8,12},{9,13},{10,... | collective-permute-start | bytes 196616 | tf_op jit(solution)/shard_map/ppermute | solution.py:50
  70.5 1.5 collective-permute-start.27
  73.3 2.1 %collective-permute-start.24 = (f32[256,128]{1,0:T(8,128)S(1)}, f32[256,128]{1,0:T(8,128)S(1)}, u32[]{:S(2)}, u32[]{:S(2)}) collective-permute-start(f32[256,128]{1,0:T(8,128)S(1)} %pad_maximum_fusion.refs_0_), channel_id=1, source_target_pairs={{0,4},{1,5},{2,6},{3,7},{4,0},{5,1},{6,2},{7,3},{8,12},{9,13},{10,... | collective-permute-start | bytes 393224 | tf_op jit(solution)/shard_map/ppermute | solution.py:50
  76.6 1.6 %collective-permute-start.29 = (f32[256,128]{1,0:T(8,128)S(1)}, f32[256,128]{1,0:T(8,128)S(1)}, u32[]{:S(2)}, u32[]{:S(2)}) collective-permute-start(f32[256,128]{1,0:T(8,128)S(1)} %collective-permute-done.28.refs_6_), channel_id=1, source_target_pairs={{0,4},{1,5},{2,6},{3,7},{4,0},{5,1},{6,2},{7,3},{8,12},{9,13},{10,... | collective-permute-start | bytes 393224 | tf_op jit(solution)/shard_map/ppermute | solution.py:50
  79.5 1.9 %collective-permute-start.26 = (f32[256,128]{1,0:T(8,128)S(1)}, f32[256,128]{1,0:T(8,128)S(1)}, u32[]{:S(2)}, u32[]{:S(2)}) collective-permute-start(f32[256,128]{1,0:T(8,128)S(1)} %collective-permute-done.24.refs_1_), channel_id=1, source_target_pairs={{0,2},{1,3},{2,0},{3,1},{4,6},{5,7},{6,4},{7,5},{8,10},{9,11},{10,... | collective-permute-start | bytes 393224 | tf_op jit(solution)/shard_map/ppermute | solution.py:50
  81.8 1.6 %collective-permute-start.37 = (f32[32,512]{1,0:T(8,128)S(1)}, f32[32,512]{1,0:T(8,128)S(1)}, u32[]{:S(2)}, u32[]{:S(2)}) collective-permute-start(f32[32,512]{1,0:T(8,128)S(1)} %get-tuple-element.93), channel_id=1, source_target_pairs={{0,6},{1,7},{2,4},{3,5},{4,2},{5,3},{6,0},{7,1},{8,14},{9,15},{10,... | collective-permute-start | bytes 196616 | tf_op jit(solution)/shard_map/ppermute | solution.py:50
  85.3 1.6 collective-permute-start.30
  87.2 2.0 %collective-permute-done.38.refs_7_ = f32[32,512]{1,0:T(8,128)S(1)} collective-permute-done((f32[32,512]{1,0:T(8,128)S(1)}, f32[32,512]{1,0:T(8,128)S(1)}, u32[]{:S(2)}, u32[]{:S(2)}) %collective-permute-start.38) | collective-permute-done | bytes 65568 | tf_op jit(solution)/shard_map/ppermute | solution.py:50
  89.7 2.1 %collective-permute-start.42 = (f32[128,128]{1,0:T(8,128)S(1)}, f32[128,128]{1,0:T(8,128)S(1)}, u32[]{:S(2)}, u32[]{:S(2)}) collective-permute-start(f32[128,128]{1,0:T(8,128)S(1)} %add.78), channel_id=1, source_target_pairs={{0,8},{1,9},{2,10},{3,11},{4,12},{5,13},{6,14},{7,15},{8,0},{9,1},... | collective-permute-start | bytes 196616 | tf_op jit(solution)/shard_map/ppermute | solution.py:50
  92.2 3.8 %collective-permute-done.42 = f32[128,128]{1,0:T(8,128)S(1)} collective-permute-done((f32[128,128]{1,0:T(8,128)S(1)}, f32[128,128]{1,0:T(8,128)S(1)}, u32[]{:S(2)}, u32[]{:S(2)}) %collective-permute-start.42) | collective-permute-done | bytes 65568 | tf_op jit(solution)/shard_map/ppermute | solution.py:50
  96.0 2.0 %collective-permute-start.44 = (f32[128,128]{1,0:T(8,128)S(1)}, f32[128,128]{1,0:T(8,128)S(1)}, u32[]{:S(2)}, u32[]{:S(2)}) collective-permute-start(f32[128,128]{1,0:T(8,128)S(1)} %add.78), channel_id=1, source_target_pairs={{0,24},{1,25},{2,26},{3,27},{4,28},{5,29},{6,30},{7,31},{8,16},{9,... | collective-permute-start | bytes 196616 | tf_op jit(solution)/shard_map/ppermute | solution.py:50
  99.0 3.1 %collective-permute-done.44 = f32[128,128]{1,0:T(8,128)S(1)} collective-permute-done((f32[128,128]{1,0:T(8,128)S(1)}, f32[128,128]{1,0:T(8,128)S(1)}, u32[]{:S(2)}, u32[]{:S(2)}) %collective-permute-start.44) | collective-permute-done | bytes 65568 | tf_op jit(solution)/shard_map/ppermute | solution.py:50
  102.1 2.5 %collective-permute-start.49 = (f32[256,128]{1,0:T(8,128)S(1)}, f32[256,128]{1,0:T(8,128)S(1)}, u32[]{:S(2)}, u32[]{:S(2)}) collective-permute-start(f32[256,128]{1,0:T(8,128)S(1)} %pad_maximum_fusion.3.refs_4_), channel_id=1, source_target_pairs={{0,2},{1,3},{2,0},{3,1},{4,6},{5,7},{6,4},{7,5},{8,10},{9,11},{10,... | collective-permute-start | bytes 393224 | tf_op jit(solution)/shard_map/ppermute | solution.py:50
  104.8 1.9 %collective-permute-start.48 = (f32[256,128]{1,0:T(8,128)S(1)}, f32[256,128]{1,0:T(8,128)S(1)}, u32[]{:S(2)}, u32[]{:S(2)}) collective-permute-start(f32[256,128]{1,0:T(8,128)S(1)} %pad_maximum_fusion.3.refs_4_), channel_id=1, source_target_pairs={{0,4},{1,5},{2,6},{3,7},{4,0},{5,1},{6,2},{7,3},{8,12},{9,13},{10,... | collective-permute-start | bytes 393224 | tf_op jit(solution)/shard_map/ppermute | solution.py:50
  106.7 2.2 %collective-permute-done.49.refs_6_ = f32[256,128]{1,0:T(8,128)S(1)} collective-permute-done((f32[256,128]{1,0:T(8,128)S(1)}, f32[256,128]{1,0:T(8,128)S(1)}, u32[]{:S(2)}, u32[]{:S(2)}) %collective-permute-start.49) | collective-permute-done | bytes 131104 | tf_op jit(solution)/shard_map/ppermute | solution.py:50
  108.9 2.1 %collective-permute-start.46 = (f32[256,128]{1,0:T(8,128)S(1)}, f32[256,128]{1,0:T(8,128)S(1)}, u32[]{:S(2)}, u32[]{:S(2)}) collective-permute-start(f32[256,128]{1,0:T(8,128)S(1)} %pad_maximum_fusion.2.refs_0_), channel_id=1, source_target_pairs={{0,2},{1,3},{2,0},{3,1},{4,6},{5,7},{6,4},{7,5},{8,10},{9,11},{10,... | collective-permute-start | bytes 393224 | tf_op jit(solution)/shard_map/ppermute | solution.py:50
  111.0 2.0 %collective-permute-start.47 = (f32[256,128]{1,0:T(8,128)S(1)}, f32[256,128]{1,0:T(8,128)S(1)}, u32[]{:S(2)}, u32[]{:S(2)}) collective-permute-start(f32[256,128]{1,0:T(8,128)S(1)} %collective-permute-done.45.refs_1_), channel_id=1, source_target_pairs={{0,2},{1,3},{2,0},{3,1},{4,6},{5,7},{6,4},{7,5},{8,10},{9,11},{10,... | collective-permute-start | bytes 393224 | tf_op jit(solution)/shard_map/ppermute | solution.py:50
  113.9 2.0 %collective-permute-done.50.refs_7_ = f32[256,128]{1,0:T(8,128)S(1)} collective-permute-done((f32[256,128]{1,0:T(8,128)S(1)}, f32[256,128]{1,0:T(8,128)S(1)}, u32[]{:S(2)}, u32[]{:S(2)}) %collective-permute-start.50) | collective-permute-done | bytes 131104 | tf_op jit(solution)/shard_map/ppermute | solution.py:50
  119.4 2.1 %collective-permute-start.54 = (f32[256,128]{1,0:T(8,128)S(1)}, f32[256,128]{1,0:T(8,128)S(1)}, u32[]{:S(2)}, u32[]{:S(2)}) collective-permute-start(f32[256,128]{1,0:T(8,128)S(1)} %get-tuple-element.105), channel_id=1, source_target_pairs={{0,2},{1,3},{2,0},{3,1},{4,6},{5,7},{6,4},{7,5},{8,10},{9,11},{10,... | collective-permute-start | bytes 393224 | tf_op jit(solution)/shard_map/ppermute | solution.py:50
  121.5 1.9 %collective-permute-start.53 = (f32[256,128]{1,0:T(8,128)S(1)}, f32[256,128]{1,0:T(8,128)S(1)}, u32[]{:S(2)}, u32[]{:S(2)}) collective-permute-start(f32[256,128]{1,0:T(8,128)S(1)} %get-tuple-element.103), channel_id=1, source_target_pairs={{0,2},{1,3},{2,0},{3,1},{4,6},{5,7},{6,4},{7,5},{8,10},{9,11},{10,... | collective-permute-start | bytes 393224 | tf_op jit(solution)/shard_map/ppermute | solution.py:50
  123.4 2.3 %collective-permute-done.54 = f32[256,128]{1,0:T(8,128)S(1)} collective-permute-done((f32[256,128]{1,0:T(8,128)S(1)}, f32[256,128]{1,0:T(8,128)S(1)}, u32[]{:S(2)}, u32[]{:S(2)}) %collective-permute-start.54) | collective-permute-done | bytes 131104 | tf_op jit(solution)/shard_map/ppermute | solution.py:50
  125.7 2.1 %collective-permute-start.55 = (f32[256,128]{1,0:T(8,128)S(1)}, f32[256,128]{1,0:T(8,128)S(1)}, u32[]{:S(2)}, u32[]{:S(2)}) collective-permute-start(f32[256,128]{1,0:T(8,128)S(1)} %add.81), channel_id=1, source_target_pairs={{0,4},{1,5},{2,6},{3,7},{4,0},{5,1},{6,2},{7,3},{8,12},{9,13},{10,... | collective-permute-start | bytes 393224 | tf_op jit(solution)/shard_map/ppermute | solution.py:50
  127.9 2.1 %collective-permute-start.58 = (f32[256,128]{1,0:T(8,128)S(1)}, f32[256,128]{1,0:T(8,128)S(1)}, u32[]{:S(2)}, u32[]{:S(2)}) collective-permute-start(f32[256,128]{1,0:T(8,128)S(1)} %add.84), channel_id=1, source_target_pairs={{0,2},{1,3},{2,0},{3,1},{4,6},{5,7},{6,4},{7,5},{8,10},{9,11},{10,... | collective-permute-start | bytes 393224 | tf_op jit(solution)/shard_map/ppermute | solution.py:50
  130.0 2.2 %collective-permute-done.55 = f32[256,128]{1,0:T(8,128)S(1)} collective-permute-done((f32[256,128]{1,0:T(8,128)S(1)}, f32[256,128]{1,0:T(8,128)S(1)}, u32[]{:S(2)}, u32[]{:S(2)}) %collective-permute-start.55) | collective-permute-done | bytes 131104 | tf_op jit(solution)/shard_map/ppermute | solution.py:50
  133.7 5.0 %collective-permute-done.59 = f32[256,128]{1,0:T(8,128)S(1)} collective-permute-done((f32[256,128]{1,0:T(8,128)S(1)}, f32[256,128]{1,0:T(8,128)S(1)}, u32[]{:S(2)}, u32[]{:S(2)}) %collective-permute-start.59) | collective-permute-done | bytes 131104 | tf_op jit(solution)/shard_map/ppermute | solution.py:50
  138.8 4.9 %collective-permute-done.60 = f32[256,128]{1,0:T(8,128)S(1)} collective-permute-done((f32[256,128]{1,0:T(8,128)S(1)}, f32[256,128]{1,0:T(8,128)S(1)}, u32[]{:S(2)}, u32[]{:S(2)}) %collective-permute-start.60) | collective-permute-done | bytes 131104 | tf_op jit(solution)/shard_map/ppermute | solution.py:50
  143.7 2.0 %collective-permute-start.65 = (f32[256,128]{1,0:T(8,128)S(1)}, f32[256,128]{1,0:T(8,128)S(1)}, u32[]{:S(2)}, u32[]{:S(2)}) collective-permute-start(f32[256,128]{1,0:T(8,128)S(1)} %pad_maximum_fusion.6.refs_4_), channel_id=1, source_target_pairs={{0,2},{1,3},{2,0},{3,1},{4,6},{5,7},{6,4},{7,5},{8,10},{9,11},{10,... | collective-permute-start | bytes 393224 | tf_op jit(solution)/shard_map/ppermute | solution.py:50
  145.8 2.0 %collective-permute-start.64 = (f32[256,128]{1,0:T(8,128)S(1)}, f32[256,128]{1,0:T(8,128)S(1)}, u32[]{:S(2)}, u32[]{:S(2)}) collective-permute-start(f32[256,128]{1,0:T(8,128)S(1)} %pad_maximum_fusion.6.refs_4_), channel_id=1, source_target_pairs={{0,4},{1,5},{2,6},{3,7},{4,0},{5,1},{6,2},{7,3},{8,12},{9,13},{10,... | collective-permute-start | bytes 393224 | tf_op jit(solution)/shard_map/ppermute | solution.py:50
  147.9 1.9 %collective-permute-done.65.refs_6_ = f32[256,128]{1,0:T(8,128)S(1)} collective-permute-done((f32[256,128]{1,0:T(8,128)S(1)}, f32[256,128]{1,0:T(8,128)S(1)}, u32[]{:S(2)}, u32[]{:S(2)}) %collective-permute-start.65) | collective-permute-done | bytes 131104 | tf_op jit(solution)/shard_map/ppermute | solution.py:50
  152.8 2.0 %collective-permute-done.66.refs_7_ = f32[256,128]{1,0:T(8,128)S(1)} collective-permute-done((f32[256,128]{1,0:T(8,128)S(1)}, f32[256,128]{1,0:T(8,128)S(1)}, u32[]{:S(2)}, u32[]{:S(2)}) %collective-permute-start.66) | collective-permute-done | bytes 131104 | tf_op jit(solution)/shard_map/ppermute | solution.py:50
  (152 shorter events, 41.9 us)
Async XLA Ops:
  2.0 25.8 %collective-permute-start = (f32[2048,128]{1,0:T(8,128)S(1)}, f32[2048,128]{1,0:T(8,128)S(1)}, u32[]{:S(2)}, u32[]{:S(2)}) collective-permute-start(f32[2048,128]{1,0:T(8,128)S(1)} %get-tuple-element.58), channel_id=1, source_target_pairs={{0,1},{1,0},{2,3},{3,2},{4,5},{5,4},{6,7},{7,6},{8,9},{9,8},{10,11... | collective-permute-start | bytes 3145736 | tf_op jit(solution)/shard_map/ppermute | solution.py:50
  4.5 5.8 %collective-permute-start.2 = (f32[32,640]{1,0:T(8,128)S(1)}, f32[32,640]{1,0:T(8,128)S(1)}, u32[]{:S(2)}, u32[]{:S(2)}) collective-permute-start(f32[32,640]{1,0:T(8,128)S(1)} %get-tuple-element.63), channel_id=1, source_target_pairs={{0,2},{1,3},{2,0},{3,1},{4,6},{5,7},{6,4},{7,5},{8,10},{9,11},{10,... | collective-permute-start | bytes 245768 | tf_op jit(solution)/shard_map/ppermute | solution.py:50
  7.4 6.3 %collective-permute-start.3 = (f32[32,640]{1,0:T(8,128)S(1)}, f32[32,640]{1,0:T(8,128)S(1)}, u32[]{:S(2)}, u32[]{:S(2)}) collective-permute-start(f32[32,640]{1,0:T(8,128)S(1)} %get-tuple-element.64), channel_id=1, source_target_pairs={{0,3},{1,2},{2,1},{3,0},{4,7},{5,6},{6,5},{7,4},{8,11},{9,10},{10,... | collective-permute-start | bytes 245768 | tf_op jit(solution)/shard_map/ppermute | solution.py:50
  7.4 6.9 %collective-permute-start.4 = (f32[32,640]{1,0:T(8,128)S(1)}, f32[32,640]{1,0:T(8,128)S(1)}, u32[]{:S(2)}, u32[]{:S(2)}) collective-permute-start(f32[32,640]{1,0:T(8,128)S(1)} %get-tuple-element.65), channel_id=1, source_target_pairs={{0,4},{1,5},{2,6},{3,7},{4,0},{5,1},{6,2},{7,3},{8,12},{9,13},{10,... | collective-permute-start | bytes 245768 | tf_op jit(solution)/shard_map/ppermute | solution.py:50
  8.9 5.6 %collective-permute-start.5 = (f32[32,640]{1,0:T(8,128)S(1)}, f32[32,640]{1,0:T(8,128)S(1)}, u32[]{:S(2)}, u32[]{:S(2)}) collective-permute-start(f32[32,640]{1,0:T(8,128)S(1)} %get-tuple-element.66), channel_id=1, source_target_pairs={{0,5},{1,4},{2,7},{3,6},{4,1},{5,0},{6,3},{7,2},{8,13},{9,12},{10,... | collective-permute-start | bytes 245768 | tf_op jit(solution)/shard_map/ppermute | solution.py:50
  10.2 5.9 %collective-permute-start.6 = (f32[32,640]{1,0:T(8,128)S(1)}, f32[32,640]{1,0:T(8,128)S(1)}, u32[]{:S(2)}, u32[]{:S(2)}) collective-permute-start(f32[32,640]{1,0:T(8,128)S(1)} %get-tuple-element.67), channel_id=1, source_target_pairs={{0,6},{1,7},{2,4},{3,5},{4,2},{5,3},{6,0},{7,1},{8,14},{9,15},{10,... | collective-permute-start | bytes 245768 | tf_op jit(solution)/shard_map/ppermute | solution.py:50
  18.8 6.2 %collective-permute-start.10 = (f32[128,128]{1,0:T(8,128)S(1)}, f32[128,128]{1,0:T(8,128)S(1)}, u32[]{:S(2)}, u32[]{:S(2)}) collective-permute-start(f32[128,128]{1,0:T(8,128)S(1)} %get-tuple-element.72), channel_id=1, source_target_pairs={{0,24},{1,25},{2,26},{3,27},{4,28},{5,29},{6,30},{7,31},{8,16},{9,... | collective-permute-start | bytes 196616 | tf_op jit(solution)/shard_map/ppermute | solution.py:50
  22.5 5.2 %collective-permute-start.9 = (f32[128,128]{1,0:T(8,128)S(1)}, f32[128,128]{1,0:T(8,128)S(1)}, u32[]{:S(2)}, u32[]{:S(2)}) collective-permute-start(f32[128,128]{1,0:T(8,128)S(1)} %get-tuple-element.71), channel_id=1, source_target_pairs={{0,16},{1,17},{2,18},{3,19},{4,20},{5,21},{6,22},{7,23},{8,24},{9,... | collective-permute-start | bytes 196616 | tf_op jit(solution)/shard_map/ppermute | solution.py:50
  29.5 6.4 %collective-permute-start.13 = (f32[256,128]{1,0:T(8,128)S(1)}, f32[256,128]{1,0:T(8,128)S(1)}, u32[]{:S(2)}, u32[]{:S(2)}) collective-permute-start(f32[256,128]{1,0:T(8,128)S(1)} %get-tuple-element.76), channel_id=1, source_target_pairs={{0,2},{1,3},{2,0},{3,1},{4,6},{5,7},{6,4},{7,5},{8,10},{9,11},{10,... | collective-permute-start | bytes 393224 | tf_op jit(solution)/shard_map/ppermute | solution.py:50
  31.6 6.4 %collective-permute-start.16 = (f32[256,128]{1,0:T(8,128)S(1)}, f32[256,128]{1,0:T(8,128)S(1)}, u32[]{:S(2)}, u32[]{:S(2)}) collective-permute-start(f32[256,128]{1,0:T(8,128)S(1)} %get-tuple-element.80), channel_id=1, source_target_pairs={{0,4},{1,5},{2,6},{3,7},{4,0},{5,1},{6,2},{7,3},{8,12},{9,13},{10,... | collective-permute-start | bytes 393224 | tf_op jit(solution)/shard_map/ppermute | solution.py:50
  32.6 7.6 %collective-permute-start.12 = (f32[256,128]{1,0:T(8,128)S(1)}, f32[256,128]{1,0:T(8,128)S(1)}, u32[]{:S(2)}, u32[]{:S(2)}) collective-permute-start(f32[256,128]{1,0:T(8,128)S(1)} %get-tuple-element.74), channel_id=1, source_target_pairs={{0,2},{1,3},{2,0},{3,1},{4,6},{5,7},{6,4},{7,5},{8,10},{9,11},{10,... | collective-permute-start | bytes 393224 | tf_op jit(solution)/shard_map/ppermute | solution.py:50
  36.0 6.0 %collective-permute-start.14 = (f32[256,128]{1,0:T(8,128)S(1)}, f32[256,128]{1,0:T(8,128)S(1)}, u32[]{:S(2)}, u32[]{:S(2)}) collective-permute-start(f32[256,128]{1,0:T(8,128)S(1)} %add.70), channel_id=1, source_target_pairs={{0,4},{1,5},{2,6},{3,7},{4,0},{5,1},{6,2},{7,3},{8,12},{9,13},{10,... | collective-permute-start | bytes 393224 | tf_op jit(solution)/shard_map/ppermute | solution.py:50
  37.6 5.8 %collective-permute-start.15 = (f32[256,128]{1,0:T(8,128)S(1)}, f32[256,128]{1,0:T(8,128)S(1)}, u32[]{:S(2)}, u32[]{:S(2)}) collective-permute-start(f32[256,128]{1,0:T(8,128)S(1)} %get-tuple-element.78), channel_id=1, source_target_pairs={{0,4},{1,5},{2,6},{3,7},{4,0},{5,1},{6,2},{7,3},{8,12},{9,13},{10,... | collective-permute-start | bytes 393224 | tf_op jit(solution)/shard_map/ppermute | solution.py:50
  38.1 5.3 %collective-permute-start.17 = (f32[256,128]{1,0:T(8,128)S(1)}, f32[256,128]{1,0:T(8,128)S(1)}, u32[]{:S(2)}, u32[]{:S(2)}) collective-permute-start(f32[256,128]{1,0:T(8,128)S(1)} %add.73), channel_id=1, source_target_pairs={{0,2},{1,3},{2,0},{3,1},{4,6},{5,7},{6,4},{7,5},{8,10},{9,11},{10,... | collective-permute-start | bytes 393224 | tf_op jit(solution)/shard_map/ppermute | solution.py:50
  43.5 6.0 %collective-permute-start.18 = (f32[128,128]{1,0:T(8,128)S(1)}, f32[128,128]{1,0:T(8,128)S(1)}, u32[]{:S(2)}, u32[]{:S(2)}) collective-permute-start(f32[128,128]{1,0:T(8,128)S(1)} %pad_maximum_fusion.7), channel_id=1, source_target_pairs={{0,8},{1,9},{2,10},{3,11},{4,12},{5,13},{6,14},{7,15},{8,0},{9,1},... | collective-permute-start | bytes 196616 | tf_op jit(solution)/shard_map/ppermute | solution.py:50
  45.2 6.0 %collective-permute-start.19 = (f32[128,128]{1,0:T(8,128)S(1)}, f32[128,128]{1,0:T(8,128)S(1)}, u32[]{:S(2)}, u32[]{:S(2)}) collective-permute-start(f32[128,128]{1,0:T(8,128)S(1)} %pad_maximum_fusion.8), channel_id=1, source_target_pairs={{0,16},{1,17},{2,18},{3,19},{4,20},{5,21},{6,22},{7,23},{8,24},{9,... | collective-permute-start | bytes 196616 | tf_op jit(solution)/shard_map/ppermute | solution.py:50
  46.5 6.1 %collective-permute-start.20 = (f32[128,128]{1,0:T(8,128)S(1)}, f32[128,128]{1,0:T(8,128)S(1)}, u32[]{:S(2)}, u32[]{:S(2)}) collective-permute-start(f32[128,128]{1,0:T(8,128)S(1)} %pad_maximum_fusion.9), channel_id=1, source_target_pairs={{0,24},{1,25},{2,26},{3,27},{4,28},{5,29},{6,30},{7,31},{8,16},{9,... | collective-permute-start | bytes 196616 | tf_op jit(solution)/shard_map/ppermute | solution.py:50
  48.6 62.4 %collective-permute-start.41 = (f32[256,2048]{1,0:T(8,128)S(1)}, f32[256,2048]{1,0:T(8,128)S(1)}, u32[]{:S(2)}, u32[]{:S(2)}) collective-permute-start(f32[256,2048]{1,0:T(8,128)S(1)} %get-tuple-element.99), channel_id=1, source_target_pairs={{0,1},{1,0},{2,3},{3,2},{4,5},{5,4},{6,7},{7,6},{8,9},{9,8},{10,11... | collective-permute-start | bytes 6291464 | tf_op jit(solution)/shard_map/ppermute | solution.py:50
  48.7 19.8 %collective-permute-start.32 = (f32[32,512]{1,0:T(8,128)S(1)}, f32[32,512]{1,0:T(8,128)S(1)}, u32[]{:S(2)}, u32[]{:S(2)}) collective-permute-start(f32[32,512]{1,0:T(8,128)S(1)} %get-tuple-element.88), channel_id=1, source_target_pairs={{0,1},{1,0},{2,3},{3,2},{4,5},{5,4},{6,7},{7,6},{8,9},{9,8},{10,11... | collective-permute-start | bytes 196616 | tf_op jit(solution)/shard_map/ppermute | solution.py:50
  49.4 21.1 %collective-permute-start.33 = (f32[32,512]{1,0:T(8,128)S(1)}, f32[32,512]{1,0:T(8,128)S(1)}, u32[]{:S(2)}, u32[]{:S(2)}) collective-permute-start(f32[32,512]{1,0:T(8,128)S(1)} %get-tuple-element.89), channel_id=1, source_target_pairs={{0,2},{1,3},{2,0},{3,1},{4,6},{5,7},{6,4},{7,5},{8,10},{9,11},{10,... | collective-permute-start | bytes 196616 | tf_op jit(solution)/shard_map/ppermute | solution.py:50
  51.3 19.3 %collective-permute-start.34 = (f32[32,512]{1,0:T(8,128)S(1)}, f32[32,512]{1,0:T(8,128)S(1)}, u32[]{:S(2)}, u32[]{:S(2)}) collective-permute-start(f32[32,512]{1,0:T(8,128)S(1)} %get-tuple-element.90), channel_id=1, source_target_pairs={{0,3},{1,2},{2,1},{3,0},{4,7},{5,6},{6,5},{7,4},{8,11},{9,10},{10,... | collective-permute-start | bytes 196616 | tf_op jit(solution)/shard_map/ppermute | solution.py:50
  56.9 5.6 %collective-permute-start.22 = (f32[128,128]{1,0:T(8,128)S(1)}, f32[128,128]{1,0:T(8,128)S(1)}, u32[]{:S(2)}, u32[]{:S(2)}) collective-permute-start(f32[128,128]{1,0:T(8,128)S(1)} %fusion.1), channel_id=1, source_target_pairs={{0,16},{1,17},{2,18},{3,19},{4,20},{5,21},{6,22},{7,23},{8,24},{9,... | collective-permute-start | bytes 196616 | tf_op jit(solution)/shard_map/ppermute | solution.py:50
  62.5 6.1 %collective-permute-start.23 = (f32[128,128]{1,0:T(8,128)S(1)}, f32[128,128]{1,0:T(8,128)S(1)}, u32[]{:S(2)}, u32[]{:S(2)}) collective-permute-start(f32[128,128]{1,0:T(8,128)S(1)} %fusion.1), channel_id=1, source_target_pairs={{0,24},{1,25},{2,26},{3,27},{4,28},{5,29},{6,30},{7,31},{8,16},{9,... | collective-permute-start | bytes 196616 | tf_op jit(solution)/shard_map/ppermute | solution.py:50
  68.5 49.0 %collective-permute-start.31 = (f32[2048,256]{1,0:T(8,128)S(1)}, f32[2048,256]{1,0:T(8,128)S(1)}, u32[]{:S(2)}, u32[]{:S(2)}) collective-permute-start(f32[2048,256]{1,0:T(8,128)S(1)} %get-tuple-element.84), channel_id=1, source_target_pairs={{0,1},{1,0},{2,3},{3,2},{4,5},{5,4},{6,7},{7,6},{8,9},{9,8},{10,11... | collective-permute-start | bytes 6291464 | tf_op jit(solution)/shard_map/ppermute | solution.py:50
  70.5 5.6 %collective-permute-start.28 = (f32[256,128]{1,0:T(8,128)S(1)}, f32[256,128]{1,0:T(8,128)S(1)}, u32[]{:S(2)}, u32[]{:S(2)}) collective-permute-start(f32[256,128]{1,0:T(8,128)S(1)} %pad_maximum_fusion.1.refs_4_), channel_id=1, source_target_pairs={{0,2},{1,3},{2,0},{3,1},{4,6},{5,7},{6,4},{7,5},{8,10},{9,11},{10,... | collective-permute-start | bytes 393224 | tf_op jit(solution)/shard_map/ppermute | solution.py:50
  70.5 6.1 %collective-permute-start.27 = (f32[256,128]{1,0:T(8,128)S(1)}, f32[256,128]{1,0:T(8,128)S(1)}, u32[]{:S(2)}, u32[]{:S(2)}) collective-permute-start(f32[256,128]{1,0:T(8,128)S(1)} %pad_maximum_fusion.1.refs_4_), channel_id=1, source_target_pairs={{0,4},{1,5},{2,6},{3,7},{4,0},{5,1},{6,2},{7,3},{8,12},{9,13},{10,... | collective-permute-start | bytes 393224 | tf_op jit(solution)/shard_map/ppermute | solution.py:50
  73.3 6.3 %collective-permute-start.24 = (f32[256,128]{1,0:T(8,128)S(1)}, f32[256,128]{1,0:T(8,128)S(1)}, u32[]{:S(2)}, u32[]{:S(2)}) collective-permute-start(f32[256,128]{1,0:T(8,128)S(1)} %pad_maximum_fusion.refs_0_), channel_id=1, source_target_pairs={{0,4},{1,5},{2,6},{3,7},{4,0},{5,1},{6,2},{7,3},{8,12},{9,13},{10,... | collective-permute-start | bytes 393224 | tf_op jit(solution)/shard_map/ppermute | solution.py:50
  76.1 5.3 %collective-permute-start.25 = (f32[256,128]{1,0:T(8,128)S(1)}, f32[256,128]{1,0:T(8,128)S(1)}, u32[]{:S(2)}, u32[]{:S(2)}) collective-permute-start(f32[256,128]{1,0:T(8,128)S(1)} %pad_maximum_fusion.refs_0_), channel_id=1, source_target_pairs={{0,2},{1,3},{2,0},{3,1},{4,6},{5,7},{6,4},{7,5},{8,10},{9,11},{10,... | collective-permute-start | bytes 393224 | tf_op jit(solution)/shard_map/ppermute | solution.py:50
  76.6 5.2 %collective-permute-start.29 = (f32[256,128]{1,0:T(8,128)S(1)}, f32[256,128]{1,0:T(8,128)S(1)}, u32[]{:S(2)}, u32[]{:S(2)}) collective-permute-start(f32[256,128]{1,0:T(8,128)S(1)} %collective-permute-done.28.refs_6_), channel_id=1, source_target_pairs={{0,4},{1,5},{2,6},{3,7},{4,0},{5,1},{6,2},{7,3},{8,12},{9,13},{10,... | collective-permute-start | bytes 393224 | tf_op jit(solution)/shard_map/ppermute | solution.py:50
  79.5 5.1 %collective-permute-start.26 = (f32[256,128]{1,0:T(8,128)S(1)}, f32[256,128]{1,0:T(8,128)S(1)}, u32[]{:S(2)}, u32[]{:S(2)}) collective-permute-start(f32[256,128]{1,0:T(8,128)S(1)} %collective-permute-done.24.refs_1_), channel_id=1, source_target_pairs={{0,2},{1,3},{2,0},{3,1},{4,6},{5,7},{6,4},{7,5},{8,10},{9,11},{10,... | collective-permute-start | bytes 393224 | tf_op jit(solution)/shard_map/ppermute | solution.py:50
  81.8 5.4 %collective-permute-start.37 = (f32[32,512]{1,0:T(8,128)S(1)}, f32[32,512]{1,0:T(8,128)S(1)}, u32[]{:S(2)}, u32[]{:S(2)}) collective-permute-start(f32[32,512]{1,0:T(8,128)S(1)} %get-tuple-element.93), channel_id=1, source_target_pairs={{0,6},{1,7},{2,4},{3,5},{4,2},{5,3},{6,0},{7,1},{8,14},{9,15},{10,... | collective-permute-start | bytes 196616 | tf_op jit(solution)/shard_map/ppermute | solution.py:50
  89.6 15.2 %collective-permute-start.39 = (f32[256,128]{1,0:T(8,128)S(1)}, f32[256,128]{1,0:T(8,128)S(1)}, u32[]{:S(2)}, u32[]{:S(2)}) collective-permute-start(f32[256,128]{1,0:T(8,128)S(1)} %get-tuple-element.97), channel_id=1, source_target_pairs={{0,8},{1,9},{2,10},{3,11},{4,12},{5,13},{6,14},{7,15},{8,0},{9,1},... | collective-permute-start | bytes 393224 | tf_op jit(solution)/shard_map/ppermute | solution.py:50
  89.7 6.3 %collective-permute-start.42 = (f32[128,128]{1,0:T(8,128)S(1)}, f32[128,128]{1,0:T(8,128)S(1)}, u32[]{:S(2)}, u32[]{:S(2)}) collective-permute-start(f32[128,128]{1,0:T(8,128)S(1)} %add.78), channel_id=1, source_target_pairs={{0,8},{1,9},{2,10},{3,11},{4,12},{5,13},{6,14},{7,15},{8,0},{9,1},... | collective-permute-start | bytes 196616 | tf_op jit(solution)/shard_map/ppermute | solution.py:50
  91.7 7.2 %collective-permute-start.43 = (f32[128,128]{1,0:T(8,128)S(1)}, f32[128,128]{1,0:T(8,128)S(1)}, u32[]{:S(2)}, u32[]{:S(2)}) collective-permute-start(f32[128,128]{1,0:T(8,128)S(1)} %add.78), channel_id=1, source_target_pairs={{0,16},{1,17},{2,18},{3,19},{4,20},{5,21},{6,22},{7,23},{8,24},{9,... | collective-permute-start | bytes 196616 | tf_op jit(solution)/shard_map/ppermute | solution.py:50
  96.0 6.1 %collective-permute-start.44 = (f32[128,128]{1,0:T(8,128)S(1)}, f32[128,128]{1,0:T(8,128)S(1)}, u32[]{:S(2)}, u32[]{:S(2)}) collective-permute-start(f32[128,128]{1,0:T(8,128)S(1)} %add.78), channel_id=1, source_target_pairs={{0,24},{1,25},{2,26},{3,27},{4,28},{5,29},{6,30},{7,31},{8,16},{9,... | collective-permute-start | bytes 196616 | tf_op jit(solution)/shard_map/ppermute | solution.py:50
  102.1 6.8 %collective-permute-start.49 = (f32[256,128]{1,0:T(8,128)S(1)}, f32[256,128]{1,0:T(8,128)S(1)}, u32[]{:S(2)}, u32[]{:S(2)}) collective-permute-start(f32[256,128]{1,0:T(8,128)S(1)} %pad_maximum_fusion.3.refs_4_), channel_id=1, source_target_pairs={{0,2},{1,3},{2,0},{3,1},{4,6},{5,7},{6,4},{7,5},{8,10},{9,11},{10,... | collective-permute-start | bytes 393224 | tf_op jit(solution)/shard_map/ppermute | solution.py:50
  104.6 6.4 %collective-permute-start.45 = (f32[256,128]{1,0:T(8,128)S(1)}, f32[256,128]{1,0:T(8,128)S(1)}, u32[]{:S(2)}, u32[]{:S(2)}) collective-permute-start(f32[256,128]{1,0:T(8,128)S(1)} %pad_maximum_fusion.2.refs_0_), channel_id=1, source_target_pairs={{0,4},{1,5},{2,6},{3,7},{4,0},{5,1},{6,2},{7,3},{8,12},{9,13},{10,... | collective-permute-start | bytes 393224 | tf_op jit(solution)/shard_map/ppermute | solution.py:50
  104.8 8.5 %collective-permute-start.48 = (f32[256,128]{1,0:T(8,128)S(1)}, f32[256,128]{1,0:T(8,128)S(1)}, u32[]{:S(2)}, u32[]{:S(2)}) collective-permute-start(f32[256,128]{1,0:T(8,128)S(1)} %pad_maximum_fusion.3.refs_4_), channel_id=1, source_target_pairs={{0,4},{1,5},{2,6},{3,7},{4,0},{5,1},{6,2},{7,3},{8,12},{9,13},{10,... | collective-permute-start | bytes 393224 | tf_op jit(solution)/shard_map/ppermute | solution.py:50
  119.4 6.3 %collective-permute-start.54 = (f32[256,128]{1,0:T(8,128)S(1)}, f32[256,128]{1,0:T(8,128)S(1)}, u32[]{:S(2)}, u32[]{:S(2)}) collective-permute-start(f32[256,128]{1,0:T(8,128)S(1)} %get-tuple-element.105), channel_id=1, source_target_pairs={{0,2},{1,3},{2,0},{3,1},{4,6},{5,7},{6,4},{7,5},{8,10},{9,11},{10,... | collective-permute-start | bytes 393224 | tf_op jit(solution)/shard_map/ppermute | solution.py:50
  121.4 6.4 %collective-permute-start.57 = (f32[256,128]{1,0:T(8,128)S(1)}, f32[256,128]{1,0:T(8,128)S(1)}, u32[]{:S(2)}, u32[]{:S(2)}) collective-permute-start(f32[256,128]{1,0:T(8,128)S(1)} %get-tuple-element.109), channel_id=1, source_target_pairs={{0,4},{1,5},{2,6},{3,7},{4,0},{5,1},{6,2},{7,3},{8,12},{9,13},{10,... | collective-permute-start | bytes 393224 | tf_op jit(solution)/shard_map/ppermute | solution.py:50
  121.5 8.4 %collective-permute-start.53 = (f32[256,128]{1,0:T(8,128)S(1)}, f32[256,128]{1,0:T(8,128)S(1)}, u32[]{:S(2)}, u32[]{:S(2)}) collective-permute-start(f32[256,128]{1,0:T(8,128)S(1)} %get-tuple-element.103), channel_id=1, source_target_pairs={{0,2},{1,3},{2,0},{3,1},{4,6},{5,7},{6,4},{7,5},{8,10},{9,11},{10,... | collective-permute-start | bytes 393224 | tf_op jit(solution)/shard_map/ppermute | solution.py:50
  125.7 6.4 %collective-permute-start.55 = (f32[256,128]{1,0:T(8,128)S(1)}, f32[256,128]{1,0:T(8,128)S(1)}, u32[]{:S(2)}, u32[]{:S(2)}) collective-permute-start(f32[256,128]{1,0:T(8,128)S(1)} %add.81), channel_id=1, source_target_pairs={{0,4},{1,5},{2,6},{3,7},{4,0},{5,1},{6,2},{7,3},{8,12},{9,13},{10,... | collective-permute-start | bytes 393224 | tf_op jit(solution)/shard_map/ppermute | solution.py:50
  127.8 5.8 %collective-permute-start.56 = (f32[256,128]{1,0:T(8,128)S(1)}, f32[256,128]{1,0:T(8,128)S(1)}, u32[]{:S(2)}, u32[]{:S(2)}) collective-permute-start(f32[256,128]{1,0:T(8,128)S(1)} %get-tuple-element.107), channel_id=1, source_target_pairs={{0,4},{1,5},{2,6},{3,7},{4,0},{5,1},{6,2},{7,3},{8,12},{9,13},{10,... | collective-permute-start | bytes 393224 | tf_op jit(solution)/shard_map/ppermute | solution.py:50
  127.9 5.7 %collective-permute-start.58 = (f32[256,128]{1,0:T(8,128)S(1)}, f32[256,128]{1,0:T(8,128)S(1)}, u32[]{:S(2)}, u32[]{:S(2)}) collective-permute-start(f32[256,128]{1,0:T(8,128)S(1)} %add.84), channel_id=1, source_target_pairs={{0,2},{1,3},{2,0},{3,1},{4,6},{5,7},{6,4},{7,5},{8,10},{9,11},{10,... | collective-permute-start | bytes 393224 | tf_op jit(solution)/shard_map/ppermute | solution.py:50
  133.6 5.0 %collective-permute-start.59 = (f32[256,128]{1,0:T(8,128)S(1)}, f32[256,128]{1,0:T(8,128)S(1)}, u32[]{:S(2)}, u32[]{:S(2)}) collective-permute-start(f32[256,128]{1,0:T(8,128)S(1)} %pad_maximum_fusion.4), channel_id=1, source_target_pairs={{0,8},{1,9},{2,10},{3,11},{4,12},{5,13},{6,14},{7,15},{8,0},{9,1},... | collective-permute-start | bytes 393224 | tf_op jit(solution)/shard_map/ppermute | solution.py:50
  143.7 6.1 %collective-permute-start.65 = (f32[256,128]{1,0:T(8,128)S(1)}, f32[256,128]{1,0:T(8,128)S(1)}, u32[]{:S(2)}, u32[]{:S(2)}) collective-permute-start(f32[256,128]{1,0:T(8,128)S(1)} %pad_maximum_fusion.6.refs_4_), channel_id=1, source_target_pairs={{0,2},{1,3},{2,0},{3,1},{4,6},{5,7},{6,4},{7,5},{8,10},{9,11},{10,... | collective-permute-start | bytes 393224 | tf_op jit(solution)/shard_map/ppermute | solution.py:50
  145.7 5.4 %collective-permute-start.61 = (f32[256,128]{1,0:T(8,128)S(1)}, f32[256,128]{1,0:T(8,128)S(1)}, u32[]{:S(2)}, u32[]{:S(2)}) collective-permute-start(f32[256,128]{1,0:T(8,128)S(1)} %pad_maximum_fusion.5.refs_0_), channel_id=1, source_target_pairs={{0,4},{1,5},{2,6},{3,7},{4,0},{5,1},{6,2},{7,3},{8,12},{9,13},{10,... | collective-permute-start | bytes 393224 | tf_op jit(solution)/shard_map/ppermute | solution.py:50
  145.8 6.4 %collective-permute-start.64 = (f32[256,128]{1,0:T(8,128)S(1)}, f32[256,128]{1,0:T(8,128)S(1)}, u32[]{:S(2)}, u32[]{:S(2)}) collective-permute-start(f32[256,128]{1,0:T(8,128)S(1)} %pad_maximum_fusion.6.refs_4_), channel_id=1, source_target_pairs={{0,4},{1,5},{2,6},{3,7},{4,0},{5,1},{6,2},{7,3},{8,12},{9,13},{10,... | collective-permute-start | bytes 393224 | tf_op jit(solution)/shard_map/ppermute | solution.py:50
  (26 other events, 138.5 us)
